TPU v7x, 512 devices: a whole 4x4x16 slice. The times are simulated.
512 devices in a mesh: dp: 16 (over z), expert: 32 (over x, y, core).
Axes of the slice: x: 4, y: 4, z: 16, core: 2. Of those that a mesh axis runs over, the one named last changes fastest.
Arguments:
- x_rows: bfloat16 [32, 2, 4096, 2048], P('expert', None, 'dp'), may hold values from -6 to 6
- dy_rows: bfloat16 [32, 2, 4096, 768], P('expert', None, 'dp'), may hold values from -6 to 6
- counts: int32 [32, 2, 16], P('expert', None, 'dp'), may hold values from 1 to 256, as said below
- host_table: int32 [32, 2], replicated, may hold values from 0 to 31, as said below
- owned: int32 [32], replicated, may hold values from 0 to 31, each once
- master: float32 [32, 2048, 768], P('expert', 'dp'), may hold values from -6 to 6
- moment1: float32 [32, 2048, 768], P('expert', 'dp'), may hold values from -6 to 6
- moment2: float32 [32, 2048, 768], P('expert', 'dp'), may hold values from 0.25 to 4
Outputs:
- new_master: float32 [32, 2048, 768], P('expert', 'dp')
- host_weights: bfloat16 [32, 2, 2048, 768], P('expert', None, 'dp')
Inputs may be any that keep to these rules, and one draw needn't show every extreme that they name: `host_table`: each expert is named by 1 to 4 host slots, never twice by one host; every expert is named. `counts`: rows past the count in a slot are padding.
All inputs are finite; a program needn't handle non-finite values.
Results may differ from a plain program's by a relative error of at most 0.0004.
Values may be sent and summed in bfloat16 or wider, within the bound.
A program may use at most 64 MiB of HBM per device.

v0:
```python
import math

import jax
import jax.numpy as jnp
from jax import lax
from jax.sharding import PartitionSpec as P


def adam_step(grad, weight, first, second):
    first_new = 0.8 * first + 0.2 * grad
    second_new = 0.95 * second + 0.05 * grad * grad
    return weight - 0.3 * (first_new / (jnp.sqrt(second_new) + 1e-08) + 0.1 * weight)


def send_hosts(pieces_bf, host_table, owned):
    count = pieces_bf.shape[0]
    piece = pieces_bf.shape[1]
    feats = pieces_bf.shape[2]
    slots = host_table.shape[1]
    pick = (owned[None, None, :] == host_table.T[:, :, None]).astype(jnp.bfloat16)
    buffer = jnp.einsum(
        "shp,pk->shk",
        pick,
        pieces_bf.reshape(count, piece * feats),
        preferred_element_type=jnp.float32,
    )
    buffer = buffer.astype(jnp.bfloat16).reshape(slots, count, piece, feats)
    arrived = lax.all_to_all(buffer, "expert", split_axis=1, concat_axis=1, tiled=True)
    return arrived.reshape(slots, count * piece, feats)[None]


def body(x_rows, dy_rows, counts, host_table, owned, master, moment1, moment2):
    slots = x_rows.shape[1]
    cap = x_rows.shape[2]
    width = x_rows.shape[3]
    feats = dy_rows.shape[3]
    n_dp = lax.axis_size("dp")
    n_ex = lax.axis_size("expert")
    block = width // n_dp
    piece = block // n_ex
    keep = lax.broadcasted_iota(jnp.int32, (slots, cap), 1) < counts[0]
    kept = jnp.where(keep[:, :, None], dy_rows[0], jnp.zeros((), jnp.bfloat16))
    columns = lax.all_to_all(x_rows[0], "dp", split_axis=2, concat_axis=1, tiled=True)
    weight_grad = jnp.einsum(
        "srd,srf->sdf",
        columns,
        lax.all_gather(kept, "dp", axis=1, tiled=True),
        preferred_element_type=jnp.float32,
    )
    received = lax.all_to_all(
        weight_grad.reshape(slots, n_ex, piece, feats),
        "expert",
        split_axis=1,
        concat_axis=1,
        tiled=True,
    )
    labels = lax.broadcasted_iota(jnp.int32, (n_ex, slots, n_ex), 0)
    assign = (host_table.T[None, :, :] == labels).astype(jnp.float32)
    merged = jnp.einsum(
        "esh,shk->ek",
        assign,
        received.reshape(slots, n_ex, piece * feats),
        precision=lax.Precision.HIGHEST,
    )
    order = (owned[:, None] == lax.broadcasted_iota(jnp.int32, (n_ex, n_ex), 1)).astype(jnp.float32)
    by_owner = jnp.einsum("pe,ek->pk", order, merged, precision=lax.Precision.HIGHEST) / math.sqrt(
        n_dp * cap
    )
    at_owner = lax.all_to_all(
        by_owner.reshape(n_ex, piece, feats), "expert", split_axis=0, concat_axis=0, tiled=True
    ).reshape(block, feats)
    new_master = adam_step(at_owner, master[0], moment1[0], moment2[0])
    pieces_bf = lax.all_to_all(
        new_master.astype(jnp.bfloat16).reshape(n_ex, piece, feats),
        "expert",
        split_axis=0,
        concat_axis=0,
        tiled=True,
    )
    host_weights = send_hosts(pieces_bf, host_table, owned)
    return (new_master[None], host_weights)


def solution(mesh):
    in_specs = (
        P("expert", None, "dp", None),
        P("expert", None, "dp", None),
        P("expert", None, "dp"),
        P(),
        P(),
        P("expert", "dp", None),
        P("expert", "dp", None),
        P("expert", "dp", None),
    )
    out_specs = (P("expert", "dp", None), P("expert", None, "dp", None))
    return jax.shard_map(body, mesh=mesh, in_specs=in_specs, out_specs=out_specs, check_vma=False)
```

profile of v0, /device:TPU:1, one launch (start us, length us, event | category | flops | bytes accessed | tf_op | source)
XLA Modules:
  0.0 333.1 jit_solution(5112172563090554601)
XLA Ops:
  7.2 0.0 all-gather.2.cloned.1.call-start
  7.2 0.7 iota_compare_fusion.4
  7.9 2.2 bitcast_select_fusion
  10.1 0.0 all-gather.2.cloned.1.call-update
  10.1 4.8 %copy.15 = bf16[1,2,256,2048]{2,1,3,0:T(2,128)(2,1)S(1)} copy(bf16[1,2,256,2048]{3,2,1,0:T(8,128)(2,1)} %param.8) | data formatting | bytes 4194304 | tf_op args[0]
  15.0 127.1 %all_to_all.38 = bf16[2,256,2048]{1,0,2:T(2,128)(2,1)S(1)} all-to-all(bf16[2,256,2048]{1,0,2:T(2,128)(2,1)S(1)} %bitcast.26), channel_id=1, replica_groups=mesh['dp'=16,'expert'=32] {'dp'}, dimensions={2} | all-to-all | bytes 4194304 | tf_op jit(solution)/shard_map/all_to_all | solution.py:43
  142.1 2.5 copy.26
  144.6 2.9 all_to_all.28
  147.5 104.3 %all-gather.2.cloned.1.call-done = bf16[2,4096,768]{2,1,0:T(8,128)(2,1)} async-done(((bf16[2,256,768]{2,1,0:T(8,128)(2,1)}), bf16[2,4096,768]{2,1,0:T(8,128)(2,1)}) %all-gather.2.cloned.1.call-update) | async-done | bytes 12582928 | tf_op jit(solution)/shard_map/all_gather | solution.py:47
  251.7 6.4 %convolution_bitcast_fusion.1 = f32[2,128,768]{2,1,0:T(8,128)S(1)} fusion(bf16[2,4096,128]{1,2,0:T(8,128)(2,1)S(1)} %all_to_all.28, bf16[2,4096,768]{2,1,0:T(8,128)(2,1)} %all-gather.2.cloned.1.call-done), kind=kOutput, calls=%fused_computation.4 | convolution fusion | flops 1610612736 | bytes 15466496 | tf_op jit(solution)/shard_map/srd,srf->sdf/dot_general | solution.py:44
  258.1 0.2 reshape.84
  258.3 0.0 copy-start.3
  258.4 0.1 copy.17
  258.4 0.0 copy-start.4
  258.4 21.6 %all_to_all.39 = f32[2,32,4,768]{3,2,0,1:T(4,128)S(1)} all-to-all(f32[2,32,4,768]{3,2,0,1:T(4,128)S(1)} %copy.17), channel_id=1, replica_groups=mesh['dp'=16,'expert'=32] {'expert'}, dimensions={1} | all-to-all | bytes 1572864 | tf_op jit(solution)/shard_map/all_to_all | solution.py:50
  280.0 0.7 reshape.92
  280.7 0.0 copy-start
  280.7 0.0 copy-done.3
  280.7 0.6 convolution_bitcast_fusion
  281.3 0.0 copy-done.4
  281.3 0.0 copy-start.1
  281.4 0.0 copy-start.2
  281.4 0.4 convolution_multiply_fusion
  281.7 0.9 reshape.86
  282.7 3.8 %all-to-all-start.2 = ((f32[32,4,768]{2,1,0:T(4,128)}), f32[32,4,768]{2,1,0:T(4,128)S(1)}, u32[]{:S(2)}, u32[]{:S(2)}) async-start(f32[32,4,768]{2,1,0:T(4,128)} %reshape.86), calls=%async_computation.2 | async-start | bytes 786432 | tf_op jit(solution)/shard_map/all_to_all | solution.py:69
  286.5 0.0 copy-done
  286.5 0.1 squeeze.14
  286.6 10.2 %all-to-all-done.2 = f32[32,4,768]{2,1,0:T(4,128)S(1)} async-done(((f32[32,4,768]{2,1,0:T(4,128)}), f32[32,4,768]{2,1,0:T(4,128)S(1)}, u32[]{:S(2)}, u32[]{:S(2)}) %all-to-all-start.2) | async-done | bytes 393248 | tf_op jit(solution)/shard_map/all_to_all | solution.py:69
  296.8 0.1 reshape.87
  297.0 0.0 copy-done.1
  297.0 0.0 copy-done.2
  297.0 1.0 broadcast_multiply_fusion.1
  298.0 0.1 mul.108
  298.1 0.1 mul.111
  298.2 0.5 subtract_convert_fusion
  298.8 11.7 %all_to_all.40 = bf16[32,4,768]{2,1,0:T(4,128)(2,1)S(1)} all-to-all(bf16[32,4,768]{2,1,0:T(4,128)(2,1)S(1)} %subtract_convert_fusion), channel_id=1, replica_groups=mesh['dp'=16,'expert'=32] {'expert'}, dimensions={0} | all-to-all | bytes 393216 | tf_op jit(solution)/shard_map/all_to_all | solution.py:73
  310.4 0.1 reshape.91
  310.6 0.3 convolution_convert_fusion
  310.9 0.3 reshape.89
  311.2 0.1 copy.19
  311.3 13.8 %all_to_all.41 = bf16[2,32,4,768]{3,2,0,1:T(4,128)(2,1)S(1)} all-to-all(bf16[2,32,4,768]{3,2,0,1:T(4,128)(2,1)S(1)} %copy.19), channel_id=1, replica_groups=mesh['dp'=16,'expert'=32] {'expert'}, dimensions={1} | all-to-all | bytes 786432 | tf_op jit(solution)/shard_map/all_to_all | solution.py:28
  325.2 0.3 copy.20
  325.5 0.8 copy.21
Async XLA Ops:
  7.2 244.6 %all-gather.2.cloned.1.call-start = ((), (), s32[]{:S(2)}) async-start(), calls=%async_computation.5 | async-start | bytes 13369344 | tf_op jit(solution)/shard_map/all_gather | solution.py:47
  258.3 22.3 %copy-start.3 = (s32[32,2]{0,1:T(2,128)S(1)}, s32[32,2]{0,1:T(2,128)}, u32[]{:S(2)}) copy-start(s32[32,2]{0,1:T(2,128)} %param.11) | copy-start | bytes 772
  258.4 22.9 %copy-start.4 = (s32[32]{0:T(128)S(1)}, s32[32]{0:T(128)}, u32[]{:S(2)}) copy-start(s32[32]{0:T(128)} %param.12) | copy-start | bytes 388
  280.7 5.9 %copy-start = (f32[1,128,768]{2,1,0:T(8,128)S(1)}, f32[1,128,768]{2,1,0:T(8,128)}, u32[]{:S(2)}) copy-start(f32[1,128,768]{2,1,0:T(8,128)} %param.13) | copy-start | bytes 1179652
  281.3 15.6 %copy-start.1 = (f32[1,128,768]{2,1,0:T(8,128)S(1)}, f32[1,128,768]{2,1,0:T(8,128)}, u32[]{:S(2)}) copy-start(f32[1,128,768]{2,1,0:T(8,128)} %param.14) | copy-start | bytes 1179652
  281.4 15.6 %copy-start.2 = (f32[1,128,768]{2,1,0:T(8,128)S(1)}, f32[1,128,768]{2,1,0:T(8,128)}, u32[]{:S(2)}) copy-start(f32[1,128,768]{2,1,0:T(8,128)} %param.15) | copy-start | bytes 1179652
  282.7 14.1 %all-to-all-start.2 = ((f32[32,4,768]{2,1,0:T(4,128)}), f32[32,4,768]{2,1,0:T(4,128)S(1)}, u32[]{:S(2)}, u32[]{:S(2)}) async-start(f32[32,4,768]{2,1,0:T(4,128)} %reshape.86), calls=%async_computation.2 | async-start | bytes 786432 | tf_op jit(solution)/shard_map/all_to_all | solution.py:69
Sparse Core Ops, SparseCore 0:
  10.2 241.4 all-gather.1
where the time goes:
time: 334 us; the launch traced here: 333 us
  blocking collectives  174 us (52%)
  waiting for transfers between devices  114 us (34%)
  local copies, waits for them, and re-layouts  14.3 us (4%)
  between operations  14.2 us (4%)
  matrix products  7.69 us (2%)
  other arithmetic  4.44 us (1%)
  starting transfers between devices  3.87 us (1%)
    all_to_all x1, blocking collectives, body(): lax.all_to_all(x_rows[0], 'dp', split_axis=2, concat_axis=1, tiled=True)  127 us
    all_gather x1, waiting for transfers between devices, body(): lax.all_gather(kept, 'dp', axis=1, tiled=True)  104 us
    all_to_all x1, blocking collectives, body(): lax.all_to_all(weight_grad.reshape(slots, n_ex, piece, feats), 'expert',...  21.6 us
    all_to_all x1, blocking collectives, send_hosts(): lax.all_to_all(buffer, 'expert', split_axis=1, concat_axis=1, tiled=True)  13.8 us
    all_to_all x1, blocking collectives, body(): lax.all_to_all(new_master.astype(jnp.bfloat16).reshape(n_ex, piece, feats...  11.7 us
    all_to_all x1, waiting for transfers between devices, body(): lax.all_to_all(by_owner.reshape(n_ex, piece, feats), 'expert', split_axis...  10.2 us
  transfers between devices with their start and end apart: 2, of which 2 were waited for; matrix products, arithmetic and copies ran while one was open for 2% of the time, Pallas kernels for 0%

commit v1 on v0

v1 whole, which is shorter than its diff:
```python
import math

import jax
import jax.numpy as jnp
from jax import lax
from jax.experimental import pallas as pl
from jax.experimental.pallas import tpu as pltpu
from jax.sharding import PartitionSpec as P

N_DP = 16
N_EX = 32
SLOTS = 2
CAP = 256
BLOCK = 128
FEATS = 768
HALF = 384
PARTS = 3
LANES = 128
CODES = SLOTS * 2 * BLOCK
CHUNK = CODES + 16
TOP = 32600.0
PER_OCTAVE = 256.0
HOPS = 8
MESH = pl.DeviceIdType.MESH
FLOWS = []
for _part in range(PARTS):
    FLOWS.append((_part, 1, 8 if _part % 2 == 0 else 7))
    FLOWS.append((_part, -1, 7 if _part % 2 == 0 else 8))


def encode(values, buf):
    peaks = []
    for s in range(SLOTS):
        peak = jnp.maximum(
            jnp.max(jnp.abs(values[s][0]), axis=0), jnp.max(jnp.abs(values[s][1]), axis=0)
        )
        peaks.append(jnp.maximum(peak, 1e-20))
    level = jnp.ceil(jnp.log2(jnp.concatenate(peaks, axis=0)) * PER_OCTAVE)
    inverse = jnp.exp2(level * (-1.0 / PER_OCTAVE)) * TOP
    buf[pl.ds(CODES, 16), :] = level.astype(jnp.int32).astype(jnp.int16)
    for s in range(SLOTS):
        for c in range(2):
            scaled = values[s][c] * inverse[8 * s : 8 * s + 8][None]
            code = jnp.floor(scaled + 0.5).astype(jnp.int32).astype(jnp.int16)
            buf[pl.ds((2 * s + c) * BLOCK, BLOCK), :] = code.reshape(BLOCK, LANES)


def scales(buf):
    level = buf[pl.ds(CODES, 16), :].astype(jnp.int32).astype(jnp.float32)
    return jnp.exp2(level * (1.0 / PER_OCTAVE)) * (1.0 / TOP)


def decode(buf, scale, s, c):
    code = buf[pl.ds((2 * s + c) * BLOCK, BLOCK), :].astype(jnp.int32).astype(jnp.float32)
    return code.reshape(16, 8, LANES) * scale[8 * s : 8 * s + 8][None]


def kernel(
    x_ref, dy_ref, counts_ref, table_ref, owned_ref, master_ref, first_ref, second_ref,
    new_ref, weights_ref,
    kept, send, recv, pick, sums, slots_in, state, fresh, hosted, new_in, hosted_in,
    ring_send, ring_recv, state_send, state_recv, sums_send, sums_recv,
    new_send, new_recv, hosted_send, hosted_recv,
):
    z = lax.axis_index("dp")
    me = lax.axis_index("expert")
    my_group = me // 2
    my_half = lax.rem(me, 2)

    barrier = pltpu.get_barrier_semaphore()
    for step in (1, N_DP - 1):
        pl.semaphore_signal(
            barrier, inc=1, device_id=(lax.rem(z + step, N_DP), me), device_id_type=MESH
        )

    def greet(d, carry):
        pl.semaphore_signal(
            barrier, inc=1, device_id=(z, lax.rem(me + d, N_EX)), device_id_type=MESH
        )
        return carry

    lax.fori_loop(1, N_EX, greet, 0)

    rows = lax.broadcasted_iota(jnp.int32, (CAP, LANES), 0)
    for s in range(SLOTS):
        live = (rows < counts_ref[s]).astype(jnp.float32)
        for part in range(PARTS):
            for c in range(2):
                at = HALF * c + LANES * part
                value = dy_ref[s, :, at : at + LANES].astype(jnp.float32) * live
                kept[part, s, :, c * LANES : (c + 1) * LANES] = value.astype(jnp.bfloat16)

    def local(part, s, target):
        columns = pl.ds(pl.multiple_of(target * BLOCK, BLOCK), BLOCK)
        product = lax.dot_general(
            x_ref[s, :, columns],
            kept[part, s],
            (((0,), (0,)), ((), ())),
            preferred_element_type=jnp.float32,
        )
        return [product[:, c * LANES : (c + 1) * LANES].reshape(16, 8, LANES) for c in range(2)]

    def ring_copy(f, k):
        return pltpu.make_async_remote_copy(
            src_ref=send.at[f, k - 1],
            dst_ref=recv.at[f, k - 1],
            send_sem=ring_send.at[f, k - 1],
            recv_sem=ring_recv.at[f, k - 1],
            device_id=(lax.rem(z + FLOWS[f][1] + N_DP, N_DP), me),
            device_id_type=MESH,
        )

    def target_of(f, k):
        _, sign, hops = FLOWS[f]
        return lax.rem(z + sign * (hops + 1 - k) + N_DP, N_DP)

    for f, (part, sign, hops) in enumerate(FLOWS):
        encode([local(part, s, target_of(f, 1)) for s in range(SLOTS)], send.at[f, 0])
    pl.semaphore_wait(barrier, N_EX - 1 + 2)
    for f in range(len(FLOWS)):
        ring_copy(f, 1).start()

    arrays = (master_ref, first_ref, second_ref)

    def share_state(d, carry):
        j = lax.rem(me + d, N_EX)
        rows_of = pl.ds(pl.multiple_of(8 * (j // 2), 8), 8)
        columns_of = pl.ds(pl.multiple_of(HALF * lax.rem(j, 2), LANES), HALF)
        for a in range(3):
            pltpu.make_async_remote_copy(
                src_ref=arrays[a].at[rows_of, columns_of],
                dst_ref=state.at[a, me],
                send_sem=state_send,
                recv_sem=state_recv,
                device_id=(z, j),
                device_id_type=MESH,
            ).start()
        return carry

    lax.fori_loop(1, N_EX, share_state, 0)
    my_rows = pl.ds(pl.multiple_of(8 * my_group, 8), 8)
    for a in range(3):
        pltpu.make_async_copy(
            arrays[a].at[my_rows, pl.ds(pl.multiple_of(HALF * my_half, LANES), HALF)],
            state.at[a, me],
            state_recv,
        ).start()

    lane = lax.broadcasted_iota(jnp.int32, (16, 8 * SLOTS * N_EX), 1)
    row = lax.broadcasted_iota(jnp.int32, (16, 8 * SLOTS * N_EX), 0)

    def fill(h, names):
        for s in range(SLOTS):
            names = jnp.where(lane // 8 == h * SLOTS + s, table_ref[h, s], names)
        return names

    names = lax.fori_loop(0, N_EX, fill, jnp.zeros_like(lane))

    def fill_pick(pair, carry):
        expert = jnp.where(row < 8, owned_ref[2 * pair], owned_ref[2 * pair + 1])
        same = jnp.where((names == expert) & (lane % 8 == row % 8), 1.0, 0.0)
        pick[pl.ds(pl.multiple_of(16 * pair, 16), 16), :] = same.astype(jnp.bfloat16)
        return carry

    lax.fori_loop(0, N_EX // 2, fill_pick, 0)

    def hop(k, carry):
        for f, (part, sign, hops) in enumerate(FLOWS):

            @pl.when(k <= hops)
            def _(f=f, part=part):
                ring_copy(f, k - 1).wait_recv()
                arrived = recv.at[f, k - 2]
                scale = scales(arrived)
                values = []
                for s in range(SLOTS):
                    own = local(part, s, target_of(f, k))
                    values.append([own[c] + decode(arrived, scale, s, c) for c in range(2)])
                encode(values, send.at[f, k - 1])
                ring_copy(f, k).start()

        return carry

    lax.fori_loop(2, HOPS + 1, hop, 0)

    for part in range(PARTS):
        ends = []
        for f in (2 * part, 2 * part + 1):
            hops = FLOWS[f][2]
            ring_copy(f, hops).wait_recv()
            ends.append(recv.at[f, hops - 1])
        end_scales = [scales(end) for end in ends]
        for s in range(SLOTS):
            own = local(part, s, z)
            for c in range(2):
                value = own[c]
                for end, scale in zip(ends, end_scales):
                    value = value + decode(end, scale, s, c)
                sums[part, :, c, s] = value

        def share_sums(d, carry, part=part):
            j = lax.rem(me + d, N_EX)
            pltpu.make_async_remote_copy(
                src_ref=sums.at[part, j // 2, lax.rem(j, 2)],
                dst_ref=slots_in.at[part, me],
                send_sem=sums_send,
                recv_sem=sums_recv.at[part],
                device_id=(z, j),
                device_id_type=MESH,
            ).start()
            return carry

        lax.fori_loop(1, N_EX, share_sums, 0)
        pltpu.make_async_copy(
            sums.at[part, my_group, my_half], slots_in.at[part, me], sums_recv.at[part]
        ).start()

    pltpu.make_async_copy(state, state, state_recv).wait()
    for part in range(PARTS):
        columns = slice(LANES * part, LANES * (part + 1))
        pltpu.make_async_copy(slots_in.at[part], slots_in.at[part], sums_recv.at[part]).wait()
        value = slots_in[part].reshape(8 * SLOTS * N_EX, LANES)
        grad = jnp.zeros((8 * N_EX, LANES), jnp.float32)
        for _ in range(3):
            piece = value.astype(jnp.bfloat16)
            value = value - piece.astype(jnp.float32)
            grad = grad + jnp.dot(pick[...], piece, preferred_element_type=jnp.float32)
        grad = grad * (1.0 / math.sqrt(N_DP * CAP))
        weight = state[0, :, :, columns].reshape(8 * N_EX, LANES)
        first = 0.8 * state[1, :, :, columns].reshape(8 * N_EX, LANES) + 0.2 * grad
        second = 0.95 * state[2, :, :, columns].reshape(8 * N_EX, LANES) + 0.05 * grad * grad
        new = weight - 0.3 * (first / (jnp.sqrt(second) + 1e-08) + 0.1 * weight)
        fresh[part] = new.reshape(N_EX, 8, LANES)
        spread = lax.dot_general(
            pick[...],
            new.astype(jnp.bfloat16),
            (((0,), (0,)), ((), ())),
            preferred_element_type=jnp.float32,
        )
        hosted[part] = spread.astype(jnp.bfloat16).reshape(N_EX, 16, LANES)
        at = pl.ds(pl.multiple_of(HALF * my_half + LANES * part, LANES), LANES)

        def share_new(d, carry, part=part, at=at):
            j = lax.rem(me + d, N_EX)
            pltpu.make_async_remote_copy(
                src_ref=fresh.at[part, j],
                dst_ref=new_in.at[my_rows, at],
                send_sem=new_send,
                recv_sem=new_recv,
                device_id=(z, j),
                device_id_type=MESH,
            ).start()
            pltpu.make_async_remote_copy(
                src_ref=hosted.at[part, j],
                dst_ref=hosted_in.at[my_group, :, at],
                send_sem=hosted_send,
                recv_sem=hosted_recv,
                device_id=(z, j),
                device_id_type=MESH,
            ).start()
            return carry

        lax.fori_loop(1, N_EX, share_new, 0)
        pltpu.make_async_copy(fresh.at[part, me], new_in.at[my_rows, at], new_recv).start()
        pltpu.make_async_copy(
            hosted.at[part, me], hosted_in.at[my_group, :, at], hosted_recv
        ).start()

    pltpu.make_async_copy(new_in, new_in, new_recv).wait()
    new_ref[...] = new_in[...]
    pltpu.make_async_copy(hosted_in, hosted_in, hosted_recv).wait()
    for pair in range(8):
        both = [hosted_in[2 * pair + i].astype(jnp.float32) for i in range(2)]
        for s in range(SLOTS):
            block = jnp.concatenate([b[8 * s : 8 * s + 8] for b in both], axis=0)
            weights_ref[s, 16 * pair : 16 * pair + 16, :] = block.astype(jnp.bfloat16)

    for f, (part, sign, hops) in enumerate(FLOWS):
        for k in range(1, hops + 1):
            ring_copy(f, k).wait_send()
    sent = state.at[:, pl.ds(0, N_EX - 1)]
    pltpu.make_async_copy(sent, sent, state_send).wait()
    sent = slots_in.at[:, pl.ds(0, N_EX - 1)]
    pltpu.make_async_copy(sent, sent, sums_send).wait()
    sent = fresh.at[:, pl.ds(0, N_EX - 1)]
    pltpu.make_async_copy(sent, sent, new_send).wait()
    sent = hosted.at[:, pl.ds(0, N_EX - 1)]
    pltpu.make_async_copy(sent, sent, hosted_send).wait()


def body(x_rows, dy_rows, counts, host_table, owned, master, moment1, moment2):
    vmem = pl.BlockSpec(memory_space=pltpu.VMEM)
    smem = pl.BlockSpec(memory_space=pltpu.SMEM)
    flows = len(FLOWS)
    dma = pltpu.SemaphoreType.DMA
    new_master, host_weights = pl.pallas_call(
        kernel,
        out_shape=(
            jax.ShapeDtypeStruct((BLOCK, FEATS), jnp.float32),
            jax.ShapeDtypeStruct((SLOTS, BLOCK, FEATS), jnp.bfloat16),
        ),
        in_specs=[vmem, vmem, smem, smem, smem, vmem, vmem, vmem],
        out_specs=(vmem, vmem),
        scratch_shapes=[
            pltpu.VMEM((PARTS, SLOTS, CAP, 2 * LANES), jnp.bfloat16),
            pltpu.VMEM((flows, HOPS, CHUNK, LANES), jnp.int16),
            pltpu.VMEM((flows, HOPS, CHUNK, LANES), jnp.int16),
            pltpu.VMEM((8 * N_EX, 8 * SLOTS * N_EX), jnp.bfloat16),
            pltpu.VMEM((PARTS, 16, 2, SLOTS, 8, LANES), jnp.float32),
            pltpu.VMEM((PARTS, N_EX, SLOTS, 8, LANES), jnp.float32),
            pltpu.VMEM((3, N_EX, 8, HALF), jnp.float32),
            pltpu.VMEM((PARTS, N_EX, 8, LANES), jnp.float32),
            pltpu.VMEM((PARTS, N_EX, 16, LANES), jnp.bfloat16),
            pltpu.VMEM((BLOCK, FEATS), jnp.float32),
            pltpu.VMEM((16, 16, FEATS), jnp.bfloat16),
            dma((flows, HOPS)),
            dma((flows, HOPS)),
            dma,
            dma,
            dma,
            dma((PARTS,)),
            dma,
            dma,
            dma,
            dma,
        ],
        compiler_params=pltpu.CompilerParams(
            collective_id=0, has_side_effects=True, vmem_limit_bytes=44 * 1024 * 1024
        ),
    )(
        x_rows[0], dy_rows[0], counts.reshape(SLOTS), host_table, owned,
        master[0], moment1[0], moment2[0],
    )
    return (new_master[None], host_weights[None])


def solution(mesh):
    in_specs = (
        P("expert", None, "dp", None),
        P("expert", None, "dp", None),
        P("expert", None, "dp"),
        P(),
        P(),
        P("expert", "dp", None),
        P("expert", "dp", None),
        P("expert", "dp", None),
    )
    out_specs = (P("expert", "dp", None), P("expert", None, "dp", None))
    return jax.shard_map(body, mesh=mesh, in_specs=in_specs, out_specs=out_specs, check_vma=False)
```

time: 334 us -> 114 us (0.34)
  blocking collectives: 174 us -> 0 us
  waiting for transfers between devices: 114 us -> 0 us
  Pallas kernels: 0 us -> 104 us
  between operations: 14.2 us -> 0.65 us
  matrix products: 7.69 us -> 0 us
  local copies, waits for them, and re-layouts: 14.3 us -> 9.27 us
  other arithmetic: 4.44 us -> 0 us
  starting transfers between devices: 3.87 us -> 0 us
    all_to_all x4 -> x0, blocking collectives: 174 us -> none  [the longest x1 127 us: body(): lax.all_to_all(x_rows[0], 'dp', split_axis=2, concat_axis=1, tiled=True)]
    all_gather x1 -> x0, waiting for transfers between devices: 104 us -> none  [body(): lax.all_gather(kept, 'dp', axis=1, tiled=True)]
    pallas_call x0 -> x1, Pallas kernels: none -> 104 us  [body(): pl.pallas_call(kernel, out_shape=(jax.ShapeDtypeStruct((BLOCK, FEATS), jn...]
    all_to_all x1 -> x0, waiting for transfers between devices: 10.2 us -> none  [body(): lax.all_to_all(by_owner.reshape(n_ex, piece, feats), 'expert', split_axis...]
    dot_general x4 -> x0, matrix products: 7.69 us -> none  [the longest x1 6.39 us: body(): jnp.einsum('srd,srf->sdf', columns, lax.all_gather(kept, 'dp', axis=1, ti...]
    all_to_all x3 -> x0, local copies, waits for them, and re-layouts: 5.7 us -> none  [the longest x2 5.4 us: body(): lax.all_to_all(x_rows[0], 'dp', split_axis=2, concat_axis=1, tiled=True)]
    all_to_all x1 -> x0, starting transfers between devices: 3.83 us -> none  [body(): lax.all_to_all(by_owner.reshape(n_ex, piece, feats), 'expert', split_axis...]
    unnamed x12 -> x17, local copies, waits for them, and re-layouts: 5.65 us -> 9.27 us
  transfers between devices with their start and end apart: 2 -> 0, of which waited for: 2 -> 0; matrix products, arithmetic and copies ran while one was open for 2% -> 0% of each run, Pallas kernels for 0% -> 0%
where the time goes in v1:
time: 114 us
  Pallas kernels  104 us (91%)
  local copies, waits for them, and re-layouts  9.27 us (8%)
    pallas_call x1, Pallas kernels, body(): pl.pallas_call(kernel, out_shape=(jax.ShapeDtypeStruct((BLOCK, FEATS), jn...  104 us
    unnamed x17, local copies, waits for them, and re-layouts  9.27 us

profile of v1, /device:TPU:1, one launch (start us, length us, event | category | flops | bytes accessed | tf_op | source)
XLA Modules:
  0.0 114.0 jit_solution(13059511505843178961)
XLA Ops:
  0.6 0.8 copy.10.table_ref
  1.4 0.0 copy-start
  1.4 1.6 %copy-done = bf16[1,2,256,2048]{3,2,1,0:T(8,128)(2,1)S(1)} copy-done((bf16[1,2,256,2048]{3,2,1,0:T(8,128)(2,1)S(1)}, bf16[1,2,256,2048]{3,2,1,0:T(8,128)(2,1)}, u32[]{:S(2)}) %copy-start) | copy-done | bytes 2097176
  3.0 0.0 copy-start.1
  3.0 1.1 copy-done.1
  4.1 0.0 copy-start.2
  4.1 1.0 copy-done.2
  5.1 0.0 copy-start.3
  5.1 1.0 copy-done.3
  6.1 0.0 copy-start.4
  6.1 1.0 copy-done.4
  7.1 0.0 copy-start.5
  7.1 0.7 copy-done.5
  7.8 0.0 copy-start.6
  7.8 0.7 copy-done.6
  8.4 104.1 %shard_map.95 = (f32[128,768]{1,0:T(8,128)S(1)}, bf16[2,128,768]{2,1,0:T(8,128)(2,1)S(1)}) custom-call(bf16[2,256,2048]{2,1,0:T(8,128)(2,1)S(1)} %bitcast.8, bf16[2,256,768]{2,1,0:T(8,128)(2,1)S(1)} %bitcast.9, s32[2]{0:T(128)S(1)} %bitcast.15, s32[32,2]{1,0:T(8,128)S(1)} %copy.10.table_ref, s32[32]{0:T(128)S(1)} %copy-done.6, f32[128,768]{1,0:T(8,128)S(1)} %bitcast.10, ...), custom_call_target="tpu_custom_call" | custom-call | tf_op jit(solution)/shard_map/pallas_call | solution.py:296
  112.6 0.7 copy.13
  113.3 0.7 copy.14
Async XLA Ops:
  1.4 1.6 %copy-start = (bf16[1,2,256,2048]{3,2,1,0:T(8,128)(2,1)S(1)}, bf16[1,2,256,2048]{3,2,1,0:T(8,128)(2,1)}, u32[]{:S(2)}) copy-start(bf16[1,2,256,2048]{3,2,1,0:T(8,128)(2,1)} %param.8) | copy-start | bytes 6291460
  3.0 1.1 copy-start.1
  4.1 1.0 copy-start.2
  5.1 1.0 copy-start.3
  6.1 1.0 copy-start.4
  7.1 0.7 copy-start.5
  7.8 0.7 copy-start.6

commit v2 on v1

v2 whole, which is shorter than its diff:
```python
import math

import jax
import jax.numpy as jnp
from jax import lax
from jax.experimental import pallas as pl
from jax.experimental.pallas import tpu as pltpu
from jax.sharding import PartitionSpec as P

N_DP = 16
N_EX = 32
SLOTS = 2
CAP = 256
WIDTH = 2048
BLOCK = 128
FEATS = 768
HALF = 384
PARTS = 3
LANES = 128
LAST = 2
HOPS = 8
TOP = 32600.0
PER_OCTAVE = 256.0
MESH = pl.DeviceIdType.MESH
FLOWS = ((0, 1, 8), (0, -1, 7), (1, 1, 7), (1, -1, 8))
LAST_FLOWS = ((LAST, 1, 8), (LAST, -1, 7))
CHUNK = 4 * BLOCK + 16
LAST_CHUNK = 2 * BLOCK + 16


def level_of(peak):
    return jnp.ceil(jnp.log2(jnp.maximum(peak, 1e-20)) * PER_OCTAVE)


def to_code(value):
    return jnp.floor(value + 0.5).astype(jnp.int32).astype(jnp.int16)


def to_float(code):
    return code.astype(jnp.int32).astype(jnp.float32)


def encode(values, buf):
    count = len(values[0])
    peaks = []
    for group in values:
        peak = jnp.max(jnp.abs(group[0]), axis=0)
        for value in group[1:]:
            peak = jnp.maximum(peak, jnp.max(jnp.abs(value), axis=0))
        peaks.append(peak)
    level = level_of(jnp.concatenate(peaks, axis=0))
    inverse = jnp.exp2(level * (-1.0 / PER_OCTAVE)) * TOP
    buf[pl.ds(2 * count * BLOCK, 16), :] = level.astype(jnp.int32).astype(jnp.int16)
    for s, group in enumerate(values):
        for c, value in enumerate(group):
            code = to_code(value * inverse[8 * s : 8 * s + 8][None])
            buf[pl.ds((count * s + c) * BLOCK, BLOCK), :] = code.reshape(BLOCK, LANES)


def scale_of(level):
    return jnp.exp2(to_float(level) * (1.0 / PER_OCTAVE)) * (1.0 / TOP)


def decode(buf, scale, count, s, c):
    code = to_float(buf[pl.ds((count * s + c) * BLOCK, BLOCK), :])
    return code.reshape(16, 8, LANES) * scale[8 * s : 8 * s + 8][None]


def kernel(
    x_hbm, dy_hbm, counts_hbm, table_hbm, owned_hbm, master_hbm, first_hbm, second_hbm,
    new_ref, weights_ref,
    x_ref, dy_ref, counts_ref, table_ref, owned_ref, mine,
    kept, send, recv, last_send, last_recv, last_own,
    early, early_inverse, level_out, level_in, early_scale, code_out, code_in,
    pick, sums, slots_in, state, fresh, hosted, new_in, hosted_in,
    load_sem, ring_send, ring_recv, last_ring_send, last_ring_recv,
    level_send, level_recv, code_send, code_recv, state_send, state_recv,
    sums_send, sums_recv, new_send, new_recv, hosted_send, hosted_recv,
):
    z = lax.axis_index("dp")
    me = lax.axis_index("expert")
    my_group = me // 2
    my_half = lax.rem(me, 2)

    loads = [
        pltpu.make_async_copy(src, dst, load_sem.at[i])
        for i, (src, dst) in enumerate(
            (
                (counts_hbm, counts_ref),
                (dy_hbm, dy_ref),
                (x_hbm, x_ref),
                (table_hbm, table_ref),
                (owned_hbm, owned_ref),
                (master_hbm, mine.at[0]),
                (first_hbm, mine.at[1]),
                (second_hbm, mine.at[2]),
            )
        )
    ]
    for load in loads:
        load.start()

    barrier = pltpu.get_barrier_semaphore()
    for step in (1, N_DP - 1):
        pl.semaphore_signal(
            barrier, inc=1, device_id=(lax.rem(z + step, N_DP), me), device_id_type=MESH
        )

    def greet(d, carry):
        pl.semaphore_signal(
            barrier, inc=1, device_id=(z, lax.rem(me + d, N_EX)), device_id_type=MESH
        )
        return carry

    lax.fori_loop(1, N_EX, greet, 0)

    loads[0].wait()
    loads[1].wait()
    rows = lax.broadcasted_iota(jnp.int32, (CAP, LANES), 0)
    for s in range(SLOTS):
        live = (rows < counts_ref[s]).astype(jnp.float32)
        for part in range(PARTS):
            for c in range(2):
                at = HALF * c + LANES * part
                value = dy_ref[s, :, at : at + LANES].astype(jnp.float32) * live
                kept[part, s, :, c * LANES : (c + 1) * LANES] = value.astype(jnp.bfloat16)
    loads[2].wait()

    def local(part, s, target):
        columns = pl.ds(pl.multiple_of(target * BLOCK, BLOCK), BLOCK)
        product = lax.dot_general(
            x_ref[s, :, columns],
            kept[part, s],
            (((0,), (0,)), ((), ())),
            preferred_element_type=jnp.float32,
        )
        return [product[:, c * LANES : (c + 1) * LANES].reshape(16, 8, LANES) for c in range(2)]

    def neighbour(sign):
        return (lax.rem(z + sign + N_DP, N_DP), me)

    def target_of(flow, k):
        _, sign, hops = flow
        return lax.rem(z + sign * (hops + 1 - k) + N_DP, N_DP)

    def ring_copy(f, k):
        return pltpu.make_async_remote_copy(
            src_ref=send.at[f, k - 1],
            dst_ref=recv.at[f, k - 1],
            send_sem=ring_send.at[f, k - 1],
            recv_sem=ring_recv.at[f, k - 1],
            device_id=neighbour(FLOWS[f][1]),
            device_id_type=MESH,
        )

    def last_copy(f, k):
        return pltpu.make_async_remote_copy(
            src_ref=last_send.at[f, k - 1],
            dst_ref=last_recv.at[f, k - 1],
            send_sem=last_ring_send.at[f, k - 1],
            recv_sem=last_ring_recv.at[f, k - 1],
            device_id=neighbour(LAST_FLOWS[f][1]),
            device_id_type=MESH,
        )

    for f, flow in enumerate(FLOWS):
        encode([local(flow[0], s, target_of(flow, 1)) for s in range(SLOTS)], send.at[f, 0])
    pl.semaphore_wait(barrier, N_EX - 1 + 2)
    for f in range(len(FLOWS)):
        ring_copy(f, 1).start()

    for s in range(SLOTS):
        for c in range(2):
            early_inverse[s, c] = jnp.zeros((16, 8, LANES), jnp.float32)

    def multiply(k, carry):
        for i, flow in enumerate(LAST_FLOWS):
            for s in range(SLOTS):
                products = local(LAST, s, target_of(flow, k))
                for c in range(2):
                    early[2 * (k - 1) + i, s, c] = products[c]
                    early_inverse[s, c] = jnp.maximum(early_inverse[s, c], jnp.abs(products[c]))
        return carry

    lax.fori_loop(1, HOPS + 1, multiply, 0)
    for c in range(2):
        levels = []
        for s in range(SLOTS):
            level = level_of(early_inverse[s, c])
            early_inverse[s, c] = jnp.exp2(level * (-1.0 / PER_OCTAVE)) * TOP
            levels.append(level)
        level_out[:, c] = jnp.concatenate(levels, axis=1).astype(jnp.int32).astype(jnp.int16)

    def share_levels(d, carry):
        j = lax.rem(me + d, N_EX)
        pltpu.make_async_remote_copy(
            src_ref=level_out.at[j // 2, lax.rem(j, 2)],
            dst_ref=level_in.at[me],
            send_sem=level_send,
            recv_sem=level_recv,
            device_id=(z, j),
            device_id_type=MESH,
        ).start()
        return carry

    lax.fori_loop(1, N_EX, share_levels, 0)
    pltpu.make_async_copy(level_out.at[my_group, my_half], level_in.at[me], level_recv).start()

    def spread_codes(k):
        both = pl.ds(2 * (k - 1), 2)
        for i in range(2):
            o = 2 * (k - 1) + i
            for c in range(2):
                codes = [
                    jnp.floor(early[o, s, c] * early_inverse[s, c] + 0.5) for s in range(SLOTS)
                ]
                code = jnp.concatenate(codes, axis=1).astype(jnp.int32).astype(jnp.int16)
                code_out[:, c, o] = code

        def share_codes(d, carry):
            j = lax.rem(me + d, N_EX)
            pltpu.make_async_remote_copy(
                src_ref=code_out.at[j // 2, lax.rem(j, 2), both],
                dst_ref=code_in.at[me, both],
                send_sem=code_send,
                recv_sem=code_recv.at[k - 1],
                device_id=(z, j),
                device_id_type=MESH,
            ).start()
            return carry

        lax.fori_loop(1, N_EX, share_codes, 0)
        pltpu.make_async_copy(
            code_out.at[my_group, my_half, both], code_in.at[me, both], code_recv.at[k - 1]
        ).start()

    def share_state(d, carry):
        j = lax.rem(me + d, N_EX)
        rows_of = pl.ds(pl.multiple_of(8 * (j // 2), 8), 8)
        columns_of = pl.ds(pl.multiple_of(HALF * lax.rem(j, 2), LANES), HALF)
        for a in range(3):
            pltpu.make_async_remote_copy(
                src_ref=mine.at[a, rows_of, columns_of],
                dst_ref=state.at[a, me],
                send_sem=state_send,
                recv_sem=state_recv,
                device_id=(z, j),
                device_id_type=MESH,
            ).start()
        return carry

    def merge_early(k):
        both = pl.ds(2 * (k - 1), 2)
        arrived = code_in.at[:, both]
        pltpu.make_async_copy(arrived, arrived, code_recv.at[k - 1]).wait()
        high = []
        low = []
        for i in range(2):
            value = to_float(code_in[:, 2 * (k - 1) + i]) * early_scale[...]
            value = value.reshape(8 * SLOTS * N_EX, LANES)
            top = value.astype(jnp.bfloat16)
            high.append(top)
            low.append((value - top.astype(jnp.float32)).astype(jnp.bfloat16))
        merged = jnp.dot(
            pick[...], jnp.concatenate(high, axis=1), preferred_element_type=jnp.float32
        ) + jnp.dot(pick[...], jnp.concatenate(low, axis=1), preferred_element_type=jnp.float32)
        return [merged[:, i * LANES : (i + 1) * LANES].reshape(2, 16, 8, LANES) for i in range(2)]

    def last_arrived(f, k):
        last_copy(f, k).wait_recv()
        buf = last_recv.at[f, k - 1]
        scale = scale_of(buf[pl.ds(2 * BLOCK, 16), :])
        return [decode(buf, scale, 1, g, 0) for g in range(2)]

    spread_codes(1)

    for load in loads[3:]:
        load.wait()
    lane = lax.broadcasted_iota(jnp.int32, (16, 8 * SLOTS * N_EX), 1)
    row = lax.broadcasted_iota(jnp.int32, (16, 8 * SLOTS * N_EX), 0)

    def fill(h, names):
        for s in range(SLOTS):
            names = jnp.where(lane // 8 == h * SLOTS + s, table_ref[s, h], names)
        return names

    names = lax.fori_loop(0, N_EX, fill, jnp.zeros_like(lane))

    def fill_pick(pair, carry):
        expert = jnp.where(row < 8, owned_ref[2 * pair], owned_ref[2 * pair + 1])
        same = jnp.where((names == expert) & (lane % 8 == row % 8), 1.0, 0.0)
        pick[pl.ds(pl.multiple_of(16 * pair, 16), 16), :] = same.astype(jnp.bfloat16)
        return carry

    lax.fori_loop(0, N_EX // 2, fill_pick, 0)

    spread_codes(2)
    lax.fori_loop(1, 5, share_state, 0)
    for a in range(3):
        pltpu.make_async_copy(
            mine.at[
                a,
                pl.ds(pl.multiple_of(8 * my_group, 8), 8),
                pl.ds(pl.multiple_of(HALF * my_half, LANES), HALF),
            ],
            state.at[a, me],
            state_recv,
        ).start()
    pltpu.make_async_copy(level_in, level_in, level_recv).wait()
    early_scale[...] = scale_of(level_in[...])
    merged = merge_early(1)
    for f in range(2):
        encode([[merged[f][g]] for g in range(2)], last_send.at[f, 0])
        last_copy(f, 1).start()

    def hop(k, carry):
        for f, flow in enumerate(FLOWS):

            @pl.when(k <= flow[2])
            def _(f=f, flow=flow):
                ring_copy(f, k - 1).wait_recv()
                arrived = recv.at[f, k - 2]
                scale = scale_of(arrived[pl.ds(4 * BLOCK, 16), :])
                values = []
                for s in range(SLOTS):
                    own = local(flow[0], s, target_of(flow, k))
                    values.append([own[c] + decode(arrived, scale, 2, s, c) for c in range(2)])
                encode(values, send.at[f, k - 1])
                ring_copy(f, k).start()

        @pl.when(k < HOPS)
        def _():
            spread_codes(k + 1)

        lax.fori_loop(4 * k - 3, jnp.minimum(4 * k + 1, N_EX), share_state, 0)

        merged = merge_early(k)
        arrived = last_arrived(0, k - 1)
        encode([[merged[0][g] + arrived[g]] for g in range(2)], last_send.at[0, k - 1])
        last_copy(0, k).start()

        @pl.when(k < HOPS)
        def _():
            arrived = last_arrived(1, k - 1)
            encode([[merged[1][g] + arrived[g]] for g in range(2)], last_send.at[1, k - 1])
            last_copy(1, k).start()

        @pl.when(k == HOPS)
        def _():
            last_own[...] = merged[1]

        return carry

    lax.fori_loop(2, HOPS + 1, hop, 0)

    for part in range(LAST):
        ends = []
        for f in (2 * part, 2 * part + 1):
            hops = FLOWS[f][2]
            ring_copy(f, hops).wait_recv()
            ends.append(recv.at[f, hops - 1])
        end_scales = [scale_of(end[pl.ds(4 * BLOCK, 16), :]) for end in ends]
        for s in range(SLOTS):
            own = local(part, s, z)
            for c in range(2):
                value = own[c]
                for end, scale in zip(ends, end_scales):
                    value = value + decode(end, scale, 2, s, c)
                sums[part, :, c, s] = value

        def share_sums(d, carry, part=part):
            j = lax.rem(me + d, N_EX)
            pltpu.make_async_remote_copy(
                src_ref=sums.at[part, j // 2, lax.rem(j, 2)],
                dst_ref=slots_in.at[part, me],
                send_sem=sums_send,
                recv_sem=sums_recv.at[part],
                device_id=(z, j),
                device_id_type=MESH,
            ).start()
            return carry

        lax.fori_loop(1, N_EX, share_sums, 0)
        pltpu.make_async_copy(
            sums.at[part, my_group, my_half], slots_in.at[part, me], sums_recv.at[part]
        ).start()

    my_rows = pl.ds(pl.multiple_of(8 * my_group, 8), 8)

    def apply(part, total):
        columns = slice(LANES * part, LANES * (part + 1))
        grad = total * (1.0 / math.sqrt(N_DP * CAP))
        weight = state[0, :, :, columns].reshape(8 * N_EX, LANES)
        first = 0.8 * state[1, :, :, columns].reshape(8 * N_EX, LANES) + 0.2 * grad
        second = 0.95 * state[2, :, :, columns].reshape(8 * N_EX, LANES) + 0.05 * grad * grad
        new = weight - 0.3 * (first / (jnp.sqrt(second) + 1e-08) + 0.1 * weight)
        fresh[part] = new.reshape(N_EX, 8, LANES)
        spread = lax.dot_general(
            pick[...],
            new.astype(jnp.bfloat16),
            (((0,), (0,)), ((), ())),
            preferred_element_type=jnp.float32,
        )
        hosted[part] = spread.astype(jnp.bfloat16).reshape(N_EX, 16, LANES)
        at = pl.ds(pl.multiple_of(HALF * my_half + LANES * part, LANES), LANES)

        def share_new(d, carry):
            j = lax.rem(me + d, N_EX)
            pltpu.make_async_remote_copy(
                src_ref=fresh.at[part, j],
                dst_ref=new_in.at[my_rows, at],
                send_sem=new_send,
                recv_sem=new_recv,
                device_id=(z, j),
                device_id_type=MESH,
            ).start()
            pltpu.make_async_remote_copy(
                src_ref=hosted.at[part, j],
                dst_ref=hosted_in.at[my_group, :, at],
                send_sem=hosted_send,
                recv_sem=hosted_recv,
                device_id=(z, j),
                device_id_type=MESH,
            ).start()
            return carry

        lax.fori_loop(1, N_EX, share_new, 0)
        pltpu.make_async_copy(fresh.at[part, me], new_in.at[my_rows, at], new_recv).start()
        pltpu.make_async_copy(
            hosted.at[part, me], hosted_in.at[my_group, :, at], hosted_recv
        ).start()

    pltpu.make_async_copy(state, state, state_recv).wait()
    up = last_arrived(0, LAST_FLOWS[0][2])
    down = last_arrived(1, LAST_FLOWS[1][2])
    total = jnp.concatenate(
        [(last_own[g] + up[g] + down[g]).reshape(BLOCK, LANES) for g in range(2)], axis=0
    )
    apply(LAST, total)

    for part in range(LAST):
        pltpu.make_async_copy(slots_in.at[part], slots_in.at[part], sums_recv.at[part]).wait()
        value = slots_in[part].reshape(8 * SLOTS * N_EX, LANES)
        total = jnp.zeros((8 * N_EX, LANES), jnp.float32)
        for _ in range(3):
            piece = value.astype(jnp.bfloat16)
            value = value - piece.astype(jnp.float32)
            total = total + jnp.dot(pick[...], piece, preferred_element_type=jnp.float32)
        apply(part, total)

    pltpu.make_async_copy(new_in, new_in, new_recv).wait()
    new_ref[...] = new_in[...]
    pltpu.make_async_copy(hosted_in, hosted_in, hosted_recv).wait()
    for pair in range(8):
        both = [hosted_in[2 * pair + i].astype(jnp.float32) for i in range(2)]
        for s in range(SLOTS):
            block = jnp.concatenate([b[8 * s : 8 * s + 8] for b in both], axis=0)
            weights_ref[s, 16 * pair : 16 * pair + 16, :] = block.astype(jnp.bfloat16)

    for f, flow in enumerate(FLOWS):
        for k in range(1, flow[2] + 1):
            ring_copy(f, k).wait_send()
    for f, flow in enumerate(LAST_FLOWS):
        for k in range(1, flow[2] + 1):
            last_copy(f, k).wait_send()
    others = pl.ds(0, N_EX - 1)
    for sent, sem in (
        (level_in.at[others], level_send),
        (code_in.at[others], code_send),
        (state.at[:, others], state_send),
        (slots_in.at[:, others], sums_send),
        (fresh.at[:, others], new_send),
        (hosted.at[:, others], hosted_send),
    ):
        pltpu.make_async_copy(sent, sent, sem).wait()


def body(x_rows, dy_rows, counts, host_table, owned, master, moment1, moment2):
    vmem = pl.BlockSpec(memory_space=pltpu.VMEM)
    hbm = pl.BlockSpec(memory_space=pltpu.HBM)
    dma = pltpu.SemaphoreType.DMA
    flows = len(FLOWS)
    new_master, host_weights = pl.pallas_call(
        kernel,
        out_shape=(
            jax.ShapeDtypeStruct((BLOCK, FEATS), jnp.float32),
            jax.ShapeDtypeStruct((SLOTS, BLOCK, FEATS), jnp.bfloat16),
        ),
        in_specs=[hbm] * 8,
        out_specs=(vmem, vmem),
        scratch_shapes=[
            pltpu.VMEM((SLOTS, CAP, WIDTH), jnp.bfloat16),
            pltpu.VMEM((SLOTS, CAP, FEATS), jnp.bfloat16),
            pltpu.SMEM((SLOTS,), jnp.int32),
            pltpu.SMEM((SLOTS, N_EX), jnp.int32),
            pltpu.SMEM((N_EX,), jnp.int32),
            pltpu.VMEM((3, BLOCK, FEATS), jnp.float32),
            pltpu.VMEM((PARTS, SLOTS, CAP, 2 * LANES), jnp.bfloat16),
            pltpu.VMEM((flows, HOPS, CHUNK, LANES), jnp.int16),
            pltpu.VMEM((flows, HOPS, CHUNK, LANES), jnp.int16),
            pltpu.VMEM((2, HOPS, LAST_CHUNK, LANES), jnp.int16),
            pltpu.VMEM((2, HOPS, LAST_CHUNK, LANES), jnp.int16),
            pltpu.VMEM((2, 16, 8, LANES), jnp.float32),
            pltpu.VMEM((2 * HOPS, SLOTS, 2, 16, 8, LANES), jnp.float32),
            pltpu.VMEM((SLOTS, 2, 16, 8, LANES), jnp.float32),
            pltpu.VMEM((16, 2, 16, LANES), jnp.int16),
            pltpu.VMEM((N_EX, 16, LANES), jnp.int16),
            pltpu.VMEM((N_EX, 16, LANES), jnp.float32),
            pltpu.VMEM((16, 2, 2 * HOPS, 16, LANES), jnp.int16),
            pltpu.VMEM((N_EX, 2 * HOPS, 16, LANES), jnp.int16),
            pltpu.VMEM((8 * N_EX, 8 * SLOTS * N_EX), jnp.bfloat16),
            pltpu.VMEM((LAST, 16, 2, SLOTS, 8, LANES), jnp.float32),
            pltpu.VMEM((LAST, N_EX, SLOTS, 8, LANES), jnp.float32),
            pltpu.VMEM((3, N_EX, 8, HALF), jnp.float32),
            pltpu.VMEM((PARTS, N_EX, 8, LANES), jnp.float32),
            pltpu.VMEM((PARTS, N_EX, 16, LANES), jnp.bfloat16),
            pltpu.VMEM((BLOCK, FEATS), jnp.float32),
            pltpu.VMEM((16, 16, FEATS), jnp.bfloat16),
            dma((8,)),
            dma((flows, HOPS)),
            dma((flows, HOPS)),
            dma((2, HOPS)),
            dma((2, HOPS)),
            dma,
            dma,
            dma,
            dma((HOPS,)),
            dma,
            dma,
            dma,
            dma((LAST,)),
            dma,
            dma,
            dma,
            dma,
        ],
        compiler_params=pltpu.CompilerParams(
            collective_id=0, has_side_effects=True, vmem_limit_bytes=62 * 1024 * 1024
        ),
    )(
        x_rows[0], dy_rows[0], counts.reshape(SLOTS), host_table.T, owned,
        master[0], moment1[0], moment2[0],
    )
    return (new_master[None], host_weights[None])


def solution(mesh):
    in_specs = (
        P("expert", None, "dp", None),
        P("expert", None, "dp", None),
        P("expert", None, "dp"),
        P(),
        P(),
        P("expert", "dp", None),
        P("expert", "dp", None),
        P("expert", "dp", None),
    )
    out_specs = (P("expert", "dp", None), P("expert", None, "dp", None))
    return jax.shard_map(body, mesh=mesh, in_specs=in_specs, out_specs=out_specs, check_vma=False)
```

time: 114 us -> 102 us (0.89)
  Pallas kernels: 104 us -> 97.4 us
  local copies, waits for them, and re-layouts: 9.27 us -> 3.53 us
    pallas_call x1, Pallas kernels: 104 us -> 97.4 us  [body(): pl.pallas_call(kernel, out_shape=(jax.ShapeDtypeStruct((BLOCK, FEATS), jn...]
    unnamed x17 -> x2, local copies, waits for them, and re-layouts: 9.27 us -> 3.53 us
where the time goes in v2:
time: 102 us
  Pallas kernels  97.4 us (95%)
  local copies, waits for them, and re-layouts  3.53 us (3%)
    pallas_call x1, Pallas kernels, body(): pl.pallas_call(kernel, out_shape=(jax.ShapeDtypeStruct((BLOCK, FEATS), jn...  97.4 us
    unnamed x2, local copies, waits for them, and re-layouts  3.53 us

profile of v2, /device:TPU:1, one launch (start us, length us, event | category | flops | bytes accessed | tf_op | source)
XLA Modules:
  0.0 101.6 jit_solution(11607324563293090172)
XLA Ops:
  0.6 97.4 %shard_map.95 = (f32[128,768]{1,0:T(8,128)}, bf16[2,128,768]{2,1,0:T(8,128)(2,1)}) custom-call(bf16[2,256,2048]{2,1,0:T(8,128)(2,1)} %bitcast.9, bf16[2,256,768]{2,1,0:T(8,128)(2,1)} %bitcast.10, s32[2]{0:T(128)} %bitcast.17, s32[2,32]{1,0:T(2,128)} %bitcast.16, s32[32]{0:T(128)} %owned_hbm.1, f32[128,768]{1,0:T(8,128)} %bitcast.11, f32[128,768]{1,0:T(8,128)} %bitcast.12, ...), custom_call_target="tpu_custom_call" | custom-call | tf_op jit(solution)/shard_map/pallas_call | solution.py:483
  98.0 1.8 %copy.12 = f32[1,128,768]{2,1,0:T(8,128)} copy(f32[1,128,768]{2,1,0:T(8,128)} %bitcast.15) | data formatting | bytes 786432
  99.8 1.8 %copy.13 = bf16[1,2,128,768]{3,2,1,0:T(8,128)(2,1)} copy(bf16[1,2,128,768]{3,2,1,0:T(8,128)(2,1)} %bitcast.14) | data formatting | bytes 786432

commit v3 on v2

--- a/solution.py
+++ b/solution.py
@@ -19,6 +19,7 @@
 LANES = 128
 LAST = 2
 HOPS = 8
+LAG = 3
 TOP = 32600.0
 PER_OCTAVE = 256.0
 MESH = pl.DeviceIdType.MESH
@@ -68,11 +69,11 @@
 
 def kernel(
     x_hbm, dy_hbm, counts_hbm, table_hbm, owned_hbm, master_hbm, first_hbm, second_hbm,
-    new_ref, weights_ref,
+    new_in, hosted_in,
     x_ref, dy_ref, counts_ref, table_ref, owned_ref, mine,
     kept, send, recv, last_send, last_recv, last_own,
     early, early_inverse, level_out, level_in, early_scale, code_out, code_in,
-    pick, sums, slots_in, state, fresh, hosted, new_in, hosted_in,
+    pick, sums, slots_in, state, fresh, hosted,
     load_sem, ring_send, ring_recv, last_ring_send, last_ring_recv,
     level_send, level_recv, code_send, code_recv, state_send, state_recv,
     sums_send, sums_recv, new_send, new_recv, hosted_send, hosted_recv,
@@ -114,17 +115,14 @@
 
     lax.fori_loop(1, N_EX, greet, 0)
 
-    loads[0].wait()
-    loads[1].wait()
-    rows = lax.broadcasted_iota(jnp.int32, (CAP, LANES), 0)
-    for s in range(SLOTS):
-        live = (rows < counts_ref[s]).astype(jnp.float32)
-        for part in range(PARTS):
+    def keep(part):
+        rows = lax.broadcasted_iota(jnp.int32, (CAP, LANES), 0)
+        for s in range(SLOTS):
+            live = (rows < counts_ref[s]).astype(jnp.float32)
             for c in range(2):
                 at = HALF * c + LANES * part
                 value = dy_ref[s, :, at : at + LANES].astype(jnp.float32) * live
                 kept[part, s, :, c * LANES : (c + 1) * LANES] = value.astype(jnp.bfloat16)
-    loads[2].wait()
 
     def local(part, s, target):
         columns = pl.ds(pl.multiple_of(target * BLOCK, BLOCK), BLOCK)
@@ -156,18 +154,23 @@
     def last_copy(f, k):
         return pltpu.make_async_remote_copy(
             src_ref=last_send.at[f, k - 1],
-            dst_ref=last_recv.at[f, k - 1],
+            dst_ref=last_recv.at[f, k],
             send_sem=last_ring_send.at[f, k - 1],
             recv_sem=last_ring_recv.at[f, k - 1],
             device_id=neighbour(LAST_FLOWS[f][1]),
             device_id_type=MESH,
         )
 
+    for load in loads[:3]:
+        load.wait()
     for f, flow in enumerate(FLOWS):
+        if f % 2 == 0:
+            keep(flow[0])
         encode([local(flow[0], s, target_of(flow, 1)) for s in range(SLOTS)], send.at[f, 0])
-    pl.semaphore_wait(barrier, N_EX - 1 + 2)
-    for f in range(len(FLOWS)):
+        if f == 0:
+            pl.semaphore_wait(barrier, N_EX - 1 + 2)
         ring_copy(f, 1).start()
+    keep(LAST)
 
     for s in range(SLOTS):
         for c in range(2):
@@ -267,11 +270,39 @@
         return [merged[:, i * LANES : (i + 1) * LANES].reshape(2, 16, 8, LANES) for i in range(2)]
 
     def last_arrived(f, k):
-        last_copy(f, k).wait_recv()
-        buf = last_recv.at[f, k - 1]
+        buf = last_recv.at[f, k]
         scale = scale_of(buf[pl.ds(2 * BLOCK, 16), :])
         return [decode(buf, scale, 1, g, 0) for g in range(2)]
 
+    def last_step(k):
+        merged = merge_early(k)
+
+        @pl.when(k > 1)
+        def _():
+            last_copy(0, k - 1).wait_recv()
+
+        arrived = last_arrived(0, k - 1)
+        encode([[merged[0][g] + arrived[g]] for g in range(2)], last_send.at[0, k - 1])
+        last_copy(0, k).start()
+
+        @pl.when(k > 1)
+        def _():
+            last_copy(1, k - 1).wait_recv()
+
+        arrived = last_arrived(1, k - 1)
+        values = [merged[1][g] + arrived[g] for g in range(2)]
+
+        @pl.when(k < HOPS)
+        def _():
+            encode([[value] for value in values], last_send.at[1, k - 1])
+            last_copy(1, k).start()
+
+        @pl.when(k == HOPS)
+        def _():
+            for g in range(2):
+                last_own[g] = values[g]
+
+    last_recv[:, 0] = jnp.zeros((2, LAST_CHUNK, LANES), jnp.int16)
     spread_codes(1)
 
     for load in loads[3:]:
@@ -294,7 +325,6 @@
 
     lax.fori_loop(0, N_EX // 2, fill_pick, 0)
 
-    spread_codes(2)
     lax.fori_loop(1, 5, share_state, 0)
     for a in range(3):
         pltpu.make_async_copy(
@@ -308,11 +338,6 @@
         ).start()
     pltpu.make_async_copy(level_in, level_in, level_recv).wait()
     early_scale[...] = scale_of(level_in[...])
-    merged = merge_early(1)
-    for f in range(2):
-        encode([[merged[f][g]] for g in range(2)], last_send.at[f, 0])
-        last_copy(f, 1).start()
-
     def hop(k, carry):
         for f, flow in enumerate(FLOWS):
 
@@ -328,32 +353,19 @@
                 encode(values, send.at[f, k - 1])
                 ring_copy(f, k).start()
 
-        @pl.when(k < HOPS)
+        spread_codes(k)
+        lax.fori_loop(4 * k - 3, jnp.minimum(4 * k + 1, N_EX), share_state, 0)
+
+        @pl.when(k > LAG)
         def _():
-            spread_codes(k + 1)
-
-        lax.fori_loop(4 * k - 3, jnp.minimum(4 * k + 1, N_EX), share_state, 0)
-
-        merged = merge_early(k)
-        arrived = last_arrived(0, k - 1)
-        encode([[merged[0][g] + arrived[g]] for g in range(2)], last_send.at[0, k - 1])
-        last_copy(0, k).start()
-
-        @pl.when(k < HOPS)
-        def _():
-            arrived = last_arrived(1, k - 1)
-            encode([[merged[1][g] + arrived[g]] for g in range(2)], last_send.at[1, k - 1])
-            last_copy(1, k).start()
-
-        @pl.when(k == HOPS)
-        def _():
-            last_own[...] = merged[1]
+            last_step(k - LAG)
 
         return carry
 
     lax.fori_loop(2, HOPS + 1, hop, 0)
 
     for part in range(LAST):
+        last_step(HOPS - LAG + 1 + part)
         ends = []
         for f in (2 * part, 2 * part + 1):
             hops = FLOWS[f][2]
@@ -431,12 +443,8 @@
         ).start()
 
     pltpu.make_async_copy(state, state, state_recv).wait()
-    up = last_arrived(0, LAST_FLOWS[0][2])
-    down = last_arrived(1, LAST_FLOWS[1][2])
-    total = jnp.concatenate(
-        [(last_own[g] + up[g] + down[g]).reshape(BLOCK, LANES) for g in range(2)], axis=0
-    )
-    apply(LAST, total)
+    for k in range(HOPS - LAG + LAST + 1, HOPS + 1):
+        last_step(k)
 
     for part in range(LAST):
         pltpu.make_async_copy(slots_in.at[part], slots_in.at[part], sums_recv.at[part]).wait()
@@ -448,14 +456,15 @@
             total = total + jnp.dot(pick[...], piece, preferred_element_type=jnp.float32)
         apply(part, total)
 
+    last_copy(0, HOPS).wait_recv()
+    up = last_arrived(0, HOPS)
+    apply(
+        LAST,
+        jnp.concatenate([(last_own[g] + up[g]).reshape(BLOCK, LANES) for g in range(2)], axis=0),
+    )
+
     pltpu.make_async_copy(new_in, new_in, new_recv).wait()
-    new_ref[...] = new_in[...]
     pltpu.make_async_copy(hosted_in, hosted_in, hosted_recv).wait()
-    for pair in range(8):
-        both = [hosted_in[2 * pair + i].astype(jnp.float32) for i in range(2)]
-        for s in range(SLOTS):
-            block = jnp.concatenate([b[8 * s : 8 * s + 8] for b in both], axis=0)
-            weights_ref[s, 16 * pair : 16 * pair + 16, :] = block.astype(jnp.bfloat16)
 
     for f, flow in enumerate(FLOWS):
         for k in range(1, flow[2] + 1):
@@ -475,19 +484,28 @@
         pltpu.make_async_copy(sent, sent, sem).wait()
 
 
+def unpack(new_in, hosted_in, new_ref, weights_ref):
+    new_ref[...] = new_in[...]
+    for pair in range(8):
+        both = [hosted_in[2 * pair + i].astype(jnp.float32) for i in range(2)]
+        for s in range(SLOTS):
+            block = jnp.concatenate([b[8 * s : 8 * s + 8] for b in both], axis=0)
+            weights_ref[s, 16 * pair : 16 * pair + 16, :] = block.astype(jnp.bfloat16)
+
+
 def body(x_rows, dy_rows, counts, host_table, owned, master, moment1, moment2):
     vmem = pl.BlockSpec(memory_space=pltpu.VMEM)
     hbm = pl.BlockSpec(memory_space=pltpu.HBM)
     dma = pltpu.SemaphoreType.DMA
     flows = len(FLOWS)
-    new_master, host_weights = pl.pallas_call(
+    new_pieces, hosted_pieces = pl.pallas_call(
         kernel,
         out_shape=(
             jax.ShapeDtypeStruct((BLOCK, FEATS), jnp.float32),
-            jax.ShapeDtypeStruct((SLOTS, BLOCK, FEATS), jnp.bfloat16),
+            jax.ShapeDtypeStruct((16, 16, FEATS), jnp.bfloat16),
         ),
         in_specs=[hbm] * 8,
-        out_specs=(vmem, vmem),
+        out_specs=(hbm, hbm),
         scratch_shapes=[
             pltpu.VMEM((SLOTS, CAP, WIDTH), jnp.bfloat16),
             pltpu.VMEM((SLOTS, CAP, FEATS), jnp.bfloat16),
@@ -499,7 +517,7 @@
             pltpu.VMEM((flows, HOPS, CHUNK, LANES), jnp.int16),
             pltpu.VMEM((flows, HOPS, CHUNK, LANES), jnp.int16),
             pltpu.VMEM((2, HOPS, LAST_CHUNK, LANES), jnp.int16),
-            pltpu.VMEM((2, HOPS, LAST_CHUNK, LANES), jnp.int16),
+            pltpu.VMEM((2, HOPS + 1, LAST_CHUNK, LANES), jnp.int16),
             pltpu.VMEM((2, 16, 8, LANES), jnp.float32),
             pltpu.VMEM((2 * HOPS, SLOTS, 2, 16, 8, LANES), jnp.float32),
             pltpu.VMEM((SLOTS, 2, 16, 8, LANES), jnp.float32),
@@ -514,8 +532,6 @@
             pltpu.VMEM((3, N_EX, 8, HALF), jnp.float32),
             pltpu.VMEM((PARTS, N_EX, 8, LANES), jnp.float32),
             pltpu.VMEM((PARTS, N_EX, 16, LANES), jnp.bfloat16),
-            pltpu.VMEM((BLOCK, FEATS), jnp.float32),
-            pltpu.VMEM((16, 16, FEATS), jnp.bfloat16),
             dma((8,)),
             dma((flows, HOPS)),
             dma((flows, HOPS)),
@@ -541,6 +557,16 @@
         x_rows[0], dy_rows[0], counts.reshape(SLOTS), host_table.T, owned,
         master[0], moment1[0], moment2[0],
     )
+    new_master, host_weights = pl.pallas_call(
+        unpack,
+        out_shape=(
+            jax.ShapeDtypeStruct((BLOCK, FEATS), jnp.float32),
+            jax.ShapeDtypeStruct((SLOTS, BLOCK, FEATS), jnp.bfloat16),
+        ),
+        in_specs=[vmem, vmem],
+        out_specs=(vmem, vmem),
+        compiler_params=pltpu.CompilerParams(vmem_limit_bytes=62 * 1024 * 1024),
+    )(new_pieces, hosted_pieces)
     return (new_master[None], host_weights[None])
 
 

time: 102 us -> 98.3 us (0.964)
  local copies, waits for them, and re-layouts: 3.53 us -> 0 us
    unnamed x2 -> x0, local copies, waits for them, and re-layouts: 3.53 us -> none
    pallas_call x0 -> x1, Pallas kernels: none -> 2.02 us  [body(): pl.pallas_call(unpack, out_shape=(jax.ShapeDtypeStruct((BLOCK, FEATS), jn...]
    pallas_call x1, Pallas kernels: 97.4 us -> 95.5 us  [body(): pl.pallas_call(kernel, out_shape=(jax.ShapeDtypeStruct((BLOCK, FEATS), jn...]
where the time goes in v3:
time: 98.3 us; the launch traced here: 98.2 us
  Pallas kernels  97.6 us (99%)
    pallas_call x1, Pallas kernels, body(): pl.pallas_call(kernel, out_shape=(jax.ShapeDtypeStruct((BLOCK, FEATS), jn...  95.5 us
    pallas_call x1, Pallas kernels, body(): pl.pallas_call(unpack, out_shape=(jax.ShapeDtypeStruct((BLOCK, FEATS), jn...  2.02 us

profile of v3, /device:TPU:1, one launch (start us, length us, event | category | flops | bytes accessed | tf_op | source)
XLA Modules:
  0.0 98.2 jit_solution(3726588532251420072)
XLA Ops:
  0.6 95.5 %shard_map.95 = (f32[128,768]{1,0:T(8,128)}, bf16[16,16,768]{2,1,0:T(8,128)(2,1)}) custom-call(bf16[2,256,2048]{2,1,0:T(8,128)(2,1)} %bitcast.9, bf16[2,256,768]{2,1,0:T(8,128)(2,1)} %bitcast.10, s32[2]{0:T(128)} %bitcast.15, s32[2,32]{1,0:T(2,128)} %bitcast.14, s32[32]{0:T(128)} %owned_hbm.1, f32[128,768]{1,0:T(8,128)} %bitcast.11, f32[128,768]{1,0:T(8,128)} %bitcast.12, ...), custom_call_target="tpu_custom_call" | custom-call | tf_op jit(solution)/shard_map/pallas_call | solution.py:501
  96.2 2.0 %shard_map.96 = (f32[128,768]{1,0:T(8,128)}, bf16[2,128,768]{2,1,0:T(8,128)(2,1)}) custom-call(f32[128,768]{1,0:T(8,128)} %get-tuple-element.6.new_in, bf16[16,16,768]{2,1,0:T(8,128)(2,1)} %get-tuple-element.7.hosted_in), custom_call_target="tpu_custom_call" | custom-call | tf_op jit(solution)/shard_map/pallas_call | solution.py:560

commit v4 on v3

--- a/solution.py
+++ b/solution.py
@@ -22,6 +22,8 @@
 LAG = 3
 TOP = 32600.0
 PER_OCTAVE = 256.0
+KNEE = 2.0
+FINE = 2000.0
 MESH = pl.DeviceIdType.MESH
 FLOWS = ((0, 1, 8), (0, -1, 7), (1, 1, 7), (1, -1, 8))
 LAST_FLOWS = ((LAST, 1, 8), (LAST, -1, 7))
@@ -65,6 +67,17 @@
 def decode(buf, scale, count, s, c):
     code = to_float(buf[pl.ds((count * s + c) * BLOCK, BLOCK), :])
     return code.reshape(16, 8, LANES) * scale[8 * s : 8 * s + 8][None]
+
+
+def compress(value):
+    code = jnp.floor(jnp.log2(1.0 + jnp.abs(value) * (1.0 / KNEE)) * FINE + 0.5)
+    return jnp.where(value < 0.0, -code, code)
+
+
+def expand(code):
+    code = to_float(code)
+    size = (jnp.exp2(jnp.abs(code) * (1.0 / FINE)) - 1.0) * KNEE
+    return jnp.where(code < 0.0, -size, size)
 
 
 def kernel(
@@ -304,6 +317,7 @@
 
     last_recv[:, 0] = jnp.zeros((2, LAST_CHUNK, LANES), jnp.int16)
     spread_codes(1)
+    spread_codes(2)
 
     for load in loads[3:]:
         load.wait()
@@ -339,6 +353,10 @@
     pltpu.make_async_copy(level_in, level_in, level_recv).wait()
     early_scale[...] = scale_of(level_in[...])
     def hop(k, carry):
+        @pl.when(k > LAG)
+        def _():
+            last_step(k - LAG)
+
         for f, flow in enumerate(FLOWS):
 
             @pl.when(k <= flow[2])
@@ -353,12 +371,11 @@
                 encode(values, send.at[f, k - 1])
                 ring_copy(f, k).start()
 
-        spread_codes(k)
+        @pl.when(k < HOPS)
+        def _():
+            spread_codes(k + 1)
+
         lax.fori_loop(4 * k - 3, jnp.minimum(4 * k + 1, N_EX), share_state, 0)
-
-        @pl.when(k > LAG)
-        def _():
-            last_step(k - LAG)
 
         return carry
 
@@ -372,13 +389,17 @@
             ring_copy(f, hops).wait_recv()
             ends.append(recv.at[f, hops - 1])
         end_scales = [scale_of(end[pl.ds(4 * BLOCK, 16), :]) for end in ends]
+        codes = [[], []]
         for s in range(SLOTS):
             own = local(part, s, z)
             for c in range(2):
                 value = own[c]
                 for end, scale in zip(ends, end_scales):
                     value = value + decode(end, scale, 2, s, c)
-                sums[part, :, c, s] = value
+                codes[c].append(compress(value))
+        for c in range(2):
+            code = jnp.concatenate(codes[c], axis=1)
+            sums[part, :, c] = code.astype(jnp.int32).astype(jnp.int16)
 
         def share_sums(d, carry, part=part):
             j = lax.rem(me + d, N_EX)
@@ -448,7 +469,7 @@
 
     for part in range(LAST):
         pltpu.make_async_copy(slots_in.at[part], slots_in.at[part], sums_recv.at[part]).wait()
-        value = slots_in[part].reshape(8 * SLOTS * N_EX, LANES)
+        value = expand(slots_in[part]).reshape(8 * SLOTS * N_EX, LANES)
         total = jnp.zeros((8 * N_EX, LANES), jnp.float32)
         for _ in range(3):
             piece = value.astype(jnp.bfloat16)
@@ -527,8 +548,8 @@
             pltpu.VMEM((16, 2, 2 * HOPS, 16, LANES), jnp.int16),
             pltpu.VMEM((N_EX, 2 * HOPS, 16, LANES), jnp.int16),
             pltpu.VMEM((8 * N_EX, 8 * SLOTS * N_EX), jnp.bfloat16),
-            pltpu.VMEM((LAST, 16, 2, SLOTS, 8, LANES), jnp.float32),
-            pltpu.VMEM((LAST, N_EX, SLOTS, 8, LANES), jnp.float32),
+            pltpu.VMEM((LAST, 16, 2, 16, LANES), jnp.int16),
+            pltpu.VMEM((LAST, N_EX, 16, LANES), jnp.int16),
             pltpu.VMEM((3, N_EX, 8, HALF), jnp.float32),
             pltpu.VMEM((PARTS, N_EX, 8, LANES), jnp.float32),
             pltpu.VMEM((PARTS, N_EX, 16, LANES), jnp.bfloat16),

time: 98.3 us -> 96 us (0.977)
  Pallas kernels: 97.6 us -> 95.2 us
    pallas_call x1, Pallas kernels: 95.5 us -> 93.2 us  [body(): pl.pallas_call(kernel, out_shape=(jax.ShapeDtypeStruct((BLOCK, FEATS), jn...]
where the time goes in v4:
time: 96 us; the launch traced here: 95.8 us
  Pallas kernels  95.2 us (99%)
    pallas_call x1, Pallas kernels, body(): pl.pallas_call(kernel, out_shape=(jax.ShapeDtypeStruct((BLOCK, FEATS), jn...  93.2 us
    pallas_call x1, Pallas kernels, body(): pl.pallas_call(unpack, out_shape=(jax.ShapeDtypeStruct((BLOCK, FEATS), jn...  2.02 us

profile of v4, /device:TPU:1, one launch (start us, length us, event | category | flops | bytes accessed | tf_op | source)
XLA Modules:
  0.0 95.8 jit_solution(69452873569414581)
XLA Ops:
  0.6 93.2 %shard_map.95 = (f32[128,768]{1,0:T(8,128)}, bf16[16,16,768]{2,1,0:T(8,128)(2,1)}) custom-call(bf16[2,256,2048]{2,1,0:T(8,128)(2,1)} %bitcast.9, bf16[2,256,768]{2,1,0:T(8,128)(2,1)} %bitcast.10, s32[2]{0:T(128)} %bitcast.15, s32[2,32]{1,0:T(2,128)} %bitcast.14, s32[32]{0:T(128)} %owned_hbm.1, f32[128,768]{1,0:T(8,128)} %bitcast.11, f32[128,768]{1,0:T(8,128)} %bitcast.12, ...), custom_call_target="tpu_custom_call" | custom-call | tf_op jit(solution)/shard_map/pallas_call | solution.py:522
  93.8 2.0 %shard_map.96 = (f32[128,768]{1,0:T(8,128)}, bf16[2,128,768]{2,1,0:T(8,128)(2,1)}) custom-call(f32[128,768]{1,0:T(8,128)} %get-tuple-element.6.new_in, bf16[16,16,768]{2,1,0:T(8,128)(2,1)} %get-tuple-element.7.hosted_in), custom_call_target="tpu_custom_call" | custom-call | tf_op jit(solution)/shard_map/pallas_call | solution.py:581

commit v5 on v4

--- a/solution.py
+++ b/solution.py
@@ -174,11 +174,13 @@
             device_id_type=MESH,
         )
 
-    for load in loads[:3]:
+    for load in loads[:2]:
         load.wait()
     for f, flow in enumerate(FLOWS):
         if f % 2 == 0:
             keep(flow[0])
+        if f == 0:
+            loads[2].wait()
         encode([local(flow[0], s, target_of(flow, 1)) for s in range(SLOTS)], send.at[f, 0])
         if f == 0:
             pl.semaphore_wait(barrier, N_EX - 1 + 2)
@@ -319,26 +321,9 @@
     spread_codes(1)
     spread_codes(2)
 
-    for load in loads[3:]:
+
+    for load in loads[5:]:
         load.wait()
-    lane = lax.broadcasted_iota(jnp.int32, (16, 8 * SLOTS * N_EX), 1)
-    row = lax.broadcasted_iota(jnp.int32, (16, 8 * SLOTS * N_EX), 0)
-
-    def fill(h, names):
-        for s in range(SLOTS):
-            names = jnp.where(lane // 8 == h * SLOTS + s, table_ref[s, h], names)
-        return names
-
-    names = lax.fori_loop(0, N_EX, fill, jnp.zeros_like(lane))
-
-    def fill_pick(pair, carry):
-        expert = jnp.where(row < 8, owned_ref[2 * pair], owned_ref[2 * pair + 1])
-        same = jnp.where((names == expert) & (lane % 8 == row % 8), 1.0, 0.0)
-        pick[pl.ds(pl.multiple_of(16 * pair, 16), 16), :] = same.astype(jnp.bfloat16)
-        return carry
-
-    lax.fori_loop(0, N_EX // 2, fill_pick, 0)
-
     lax.fori_loop(1, 5, share_state, 0)
     for a in range(3):
         pltpu.make_async_copy(
@@ -350,8 +335,29 @@
             state.at[a, me],
             state_recv,
         ).start()
-    pltpu.make_async_copy(level_in, level_in, level_recv).wait()
-    early_scale[...] = scale_of(level_in[...])
+    def prepare():
+        for load in loads[3:5]:
+            load.wait()
+        lane = lax.broadcasted_iota(jnp.int32, (16, 8 * SLOTS * N_EX), 1)
+        row = lax.broadcasted_iota(jnp.int32, (16, 8 * SLOTS * N_EX), 0)
+
+        def fill(h, names):
+            for s in range(SLOTS):
+                names = jnp.where(lane // 8 == h * SLOTS + s, table_ref[s, h], names)
+            return names
+
+        names = lax.fori_loop(0, N_EX, fill, jnp.zeros_like(lane))
+
+        def fill_pick(pair, carry):
+            expert = jnp.where(row < 8, owned_ref[2 * pair], owned_ref[2 * pair + 1])
+            same = jnp.where((names == expert) & (lane % 8 == row % 8), 1.0, 0.0)
+            pick[pl.ds(pl.multiple_of(16 * pair, 16), 16), :] = same.astype(jnp.bfloat16)
+            return carry
+
+        lax.fori_loop(0, N_EX // 2, fill_pick, 0)
+        pltpu.make_async_copy(level_in, level_in, level_recv).wait()
+        early_scale[...] = scale_of(level_in[...])
+
     def hop(k, carry):
         @pl.when(k > LAG)
         def _():
@@ -377,26 +383,36 @@
 
         lax.fori_loop(4 * k - 3, jnp.minimum(4 * k + 1, N_EX), share_state, 0)
 
+        @pl.when(k == 2)
+        def _():
+            prepare()
+
         return carry
 
     lax.fori_loop(2, HOPS + 1, hop, 0)
 
+    last_step(HOPS - LAG + 1)
     for part in range(LAST):
-        last_step(HOPS - LAG + 1 + part)
-        ends = []
-        for f in (2 * part, 2 * part + 1):
-            hops = FLOWS[f][2]
-            ring_copy(f, hops).wait_recv()
-            ends.append(recv.at[f, hops - 1])
-        end_scales = [scale_of(end[pl.ds(4 * BLOCK, 16), :]) for end in ends]
-        codes = [[], []]
+        f = 2 * part if FLOWS[2 * part][2] < HOPS else 2 * part + 1
+        ring_copy(f, HOPS - 1).wait_recv()
+        end = recv.at[f, HOPS - 2]
+        scale = scale_of(end[pl.ds(4 * BLOCK, 16), :])
         for s in range(SLOTS):
             own = local(part, s, z)
             for c in range(2):
-                value = own[c]
-                for end, scale in zip(ends, end_scales):
-                    value = value + decode(end, scale, 2, s, c)
-                codes[c].append(compress(value))
+                early[part, s, c] = own[c] + decode(end, scale, 2, s, c)
+
+    for part in range(LAST):
+        if part == 1 and LAG > 2:
+            last_step(HOPS - LAG + 2)
+        f = 2 * part if FLOWS[2 * part][2] == HOPS else 2 * part + 1
+        ring_copy(f, HOPS).wait_recv()
+        end = recv.at[f, HOPS - 1]
+        scale = scale_of(end[pl.ds(4 * BLOCK, 16), :])
+        codes = [
+            [compress(early[part, s, c] + decode(end, scale, 2, s, c)) for s in range(SLOTS)]
+            for c in range(2)
+        ]
         for c in range(2):
             code = jnp.concatenate(codes[c], axis=1)
             sums[part, :, c] = code.astype(jnp.int32).astype(jnp.int16)
@@ -471,7 +487,7 @@
         pltpu.make_async_copy(slots_in.at[part], slots_in.at[part], sums_recv.at[part]).wait()
         value = expand(slots_in[part]).reshape(8 * SLOTS * N_EX, LANES)
         total = jnp.zeros((8 * N_EX, LANES), jnp.float32)
-        for _ in range(3):
+        for _ in range(2):
             piece = value.astype(jnp.bfloat16)
             value = value - piece.astype(jnp.float32)
             total = total + jnp.dot(pick[...], piece, preferred_element_type=jnp.float32)

time: 96 us -> 92.2 us (0.960)
  Pallas kernels: 95.2 us -> 91.4 us
    pallas_call x1, Pallas kernels: 93.2 us -> 89.4 us  [body(): pl.pallas_call(kernel, out_shape=(jax.ShapeDtypeStruct((BLOCK, FEATS), jn...]
where the time goes in v5:
time: 92.2 us; the launch traced here: 92 us
  Pallas kernels  91.4 us (99%)
    pallas_call x1, Pallas kernels, body(): pl.pallas_call(kernel, out_shape=(jax.ShapeDtypeStruct((BLOCK, FEATS), jn...  89.4 us
    pallas_call x1, Pallas kernels, body(): pl.pallas_call(unpack, out_shape=(jax.ShapeDtypeStruct((BLOCK, FEATS), jn...  2.02 us

profile of v5, /device:TPU:1, one launch (start us, length us, event | category | flops | bytes accessed | tf_op | source)
XLA Modules:
  0.0 92.0 jit_solution(17216042428099042646)
XLA Ops:
  0.6 89.4 %shard_map.95 = (f32[128,768]{1,0:T(8,128)}, bf16[16,16,768]{2,1,0:T(8,128)(2,1)}) custom-call(bf16[2,256,2048]{2,1,0:T(8,128)(2,1)} %bitcast.9, bf16[2,256,768]{2,1,0:T(8,128)(2,1)} %bitcast.10, s32[2]{0:T(128)} %bitcast.15, s32[2,32]{1,0:T(2,128)} %bitcast.14, s32[32]{0:T(128)} %owned_hbm.1, f32[128,768]{1,0:T(8,128)} %bitcast.11, f32[128,768]{1,0:T(8,128)} %bitcast.12, ...), custom_call_target="tpu_custom_call" | custom-call | tf_op jit(solution)/shard_map/pallas_call | solution.py:538
  90.0 2.0 %shard_map.96 = (f32[128,768]{1,0:T(8,128)}, bf16[2,128,768]{2,1,0:T(8,128)(2,1)}) custom-call(f32[128,768]{1,0:T(8,128)} %get-tuple-element.6.new_in, bf16[16,16,768]{2,1,0:T(8,128)(2,1)} %get-tuple-element.7.hosted_in), custom_call_target="tpu_custom_call" | custom-call | tf_op jit(solution)/shard_map/pallas_call | solution.py:597
